TPU v7x, 32 devices: a whole 2x2x4 slice. The times are simulated.
32 devices in a mesh: parts: 2 (over x), rows: 16 (over z, y, core).
Axes of the slice: x: 2, y: 2, z: 4, core: 2. Of those that a mesh axis runs over, the one named last changes fastest.
Arguments:
- rhs: float32 [3, 12288, 256], P(None, 'rows', 'parts'), parts along dimension 2, may hold values from -6 to 6
- diag_inv: float32 [3, 12288, 768], P(None, 'rows'), may hold values from -0.21875 to 0.21875
- tiles: float32 [2, 32, 768, 768], P(None, 'rows'), may hold values from -0.15625 to 0.15625
- dest: int32 [2, 16, 2], P(None, 'rows'), may hold values from 0 to 15, all different within a row; in each aligned block of 16 rows (0 to 15, 16 to 31, ..., all dimensions but the last counted through in order) at most 4 rows name the same one
- obs_weight: float32 [12288], P('rows'), may hold values from -0.108253175 to 0.108253175, as said below
Outputs:
- solution: float32 [3, 12288, 256], P(None, 'rows', 'parts'), parts along dimension 2
- observed: float32 [256], P('parts'), parts along dimension 0
There are 2 independent parts, one for each index of `parts`. A program takes and returns all parts, laid end to end along the dimension named above; an argument that names none is the same for every part. Nothing has to cross between parts.
Inputs may be any that keep to these rules, and one draw needn't show every extreme that they name: `dest`: in each of the two levels, the two entries of a supernode differ, and no supernode of the next level is named more than 4 times. `obs_weight`: finite weights.
All inputs are finite; a program needn't handle non-finite values.
Results may differ from a plain program's by a relative error of at most 0.00029.
Values sent between devices are 32-bit elements; how exact they have to be, the bound alone decides.
A program may use at most 128 MiB of HBM per device.

v0:
```python
import jax
import jax.numpy as jnp
from jax import lax
from jax.sharding import PartitionSpec as P


def collect_updates(solved_block, tiles_level, pattern_level):
    products = jnp.einsum(
        "kab,bc->kac",
        tiles_level,
        solved_block,
        precision=lax.Precision.HIGHEST,
        preferred_element_type=jnp.float32,
    )
    block_rows = solved_block.shape[0]
    width = products.shape[2]
    count = lax.axis_size("rows")
    sliced = lax.all_to_all(products, "rows", split_axis=1, concat_axis=0, tiled=True)
    owners = jnp.arange(count, dtype=jnp.int32)
    flat_targets = pattern_level.reshape(-1)
    matches = (owners[:, None] == flat_targets[None, :]).astype(jnp.float32)
    partial_value = jnp.einsum("mq,qac->mac", matches, sliced, precision=lax.Precision.HIGHEST)
    returned = lax.all_to_all(partial_value, "rows", split_axis=0, concat_axis=0, tiled=True)
    return returned.reshape(block_rows, width)


def body(rhs, diag_inv, tiles, dest, obs_weight):
    pattern = lax.all_gather(dest, "rows", axis=1, tiled=True)
    current = rhs[0]
    solved_levels = []
    solved_block = current
    for section in range(3):
        solved_block = jnp.dot(
            diag_inv[section],
            current,
            precision=lax.Precision.HIGHEST,
            preferred_element_type=jnp.float32,
        )
        solved_levels.append(solved_block)
        if section < 2:
            current = rhs[section + 1] - collect_updates(
                solved_block, tiles[section], pattern[section]
            )
    partial_sum = jnp.dot(
        obs_weight,
        solved_block,
        precision=lax.Precision.HIGHEST,
        preferred_element_type=jnp.float32,
    )
    observed = lax.psum(partial_sum, "rows")
    return (jnp.stack(solved_levels), observed)


def solution(mesh):
    in_specs = (
        P(None, "rows", "parts"),
        P(None, "rows", None),
        P(None, "rows", None, None),
        P(None, "rows", None),
        P("rows"),
    )
    out_specs = (P(None, "rows", "parts"), P("parts"))
    return jax.shard_map(body, mesh=mesh, in_specs=in_specs, out_specs=out_specs, check_vma=False)
```

profile of v0, /device:TPU:0, one launch (start us, length us, event | category | flops | bytes accessed | tf_op | source)
XLA Modules:
  0.0 156.7 jit_solution(14306570408259959369)
XLA Ops:
  0.6 3.7 %fusion.10 = f32[768,128]{1,0:T(8,128)S(1)} fusion(f32[3,768,768]{2,1,0:T(8,128)} %param.6, f32[3,768,128]{2,1,0:T(8,128)} %param.5), kind=kOutput, calls=%fused_computation.10 | convolution fusion | flops 905969664 | bytes 3145728 | tf_op jit(solution)/shard_map/dot_general | solution.py:33
  4.3 7.4 %fusion.15 = f32[2,768,128]{1,2,0:T(8,128)S(1)} fusion(f32[2,2,768,768]{3,2,1,0:T(8,128)} %param.7, f32[768,128]{1,0:T(8,128)S(1)} %fusion.10), kind=kOutput, calls=%fused_computation.15 | convolution fusion | flops 1811939328 | bytes 5898240 | tf_op jit(solution)/shard_map/kab,bc->kac/dot_general | solution.py:8
  11.7 0.0 copy-start.3
  11.7 1.2 copy.23
  12.9 0.0 copy-start.1
  12.9 7.5 %all-to-all-start = ((f32[2,768,128]{2,0,1:T(2,128)}), f32[2,768,128]{2,0,1:T(2,128)S(1)}, u32[]{:S(2)}, u32[]{:S(2)}) async-start(f32[2,768,128]{2,0,1:T(2,128)} %copy.23), calls=%async_computation | async-start | bytes 1572864 | tf_op jit(solution)/shard_map/all_to_all | solution.py:18
  20.4 0.0 copy-done.3
  20.4 29.2 %all_gather.3 = s32[2,16,2]{2,0,1:T(2,128)S(1)} all-gather(s32[2,1,2]{2,0,1:T(2,128)S(1)} %bitcast.82), channel_id=1, replica_groups=mesh['parts'=2,'rows'=16] {'rows'}, dimensions={1}, use_global_device_ids=true | all-gather | bytes 272 | tf_op jit(solution)/shard_map/all_gather | solution.py:28
  49.6 0.1 eq.31
  49.7 0.0 all-to-all-done
  49.7 0.0 copy-start
  49.7 0.1 copy.24
  49.8 0.6 copy.25
  50.4 0.4 fusion.29
  50.8 0.1 copy.26
  50.9 16.8 %all_to_all.46 = f32[16,48,128]{2,1,0:T(8,128)S(1)} all-to-all(f32[16,48,128]{2,1,0:T(8,128)S(1)} %copy.26), channel_id=1, replica_groups=mesh['parts'=2,'rows'=16] {'rows'}, dimensions={0} | all-to-all | bytes 786432 | tf_op jit(solution)/shard_map/all_to_all | solution.py:23
  67.7 0.0 copy-done.1
  67.7 0.1 bitcast_subtract_fusion.1
  67.8 3.8 %fusion.8 = f32[128,768]{1,0:T(8,128)S(1)} fusion(f32[3,768,768]{2,1,0:T(8,128)} %param.6, f32[1,768,128]{2,1,0:T(8,128)S(1)} %bitcast_subtract_fusion.1), kind=kOutput, calls=%fused_computation.8 | convolution fusion | flops 905969664 | bytes 3145728 | tf_op jit(solution)/shard_map/dot_general | solution.py:33
  71.5 0.0 copy-done
  71.5 5.0 %fusion.18 = f32[2,768,128]{1,2,0:T(8,128)S(1)} fusion(f32[2,2,768,768]{3,2,1,0:T(8,128)S(1)} %copy-done, f32[128,768]{1,0:T(8,128)S(1)} %fusion.8), kind=kOutput, calls=%fused_computation.16 | convolution fusion | flops 1811939328 | bytes 5898240 | tf_op jit(solution)/shard_map/kab,bc->kac/dot_general | solution.py:8
  76.5 1.2 copy.28
  77.7 3.6 %all-to-all-start.2 = ((f32[2,768,128]{2,0,1:T(2,128)}), f32[2,768,128]{2,0,1:T(2,128)S(1)}, u32[]{:S(2)}, u32[]{:S(2)}) async-start(f32[2,768,128]{2,0,1:T(2,128)} %copy.28), calls=%async_computation.2 | async-start | bytes 1572864 | tf_op jit(solution)/shard_map/all_to_all | solution.py:18
  81.3 0.1 eq.35
  81.4 18.6 %all-to-all-done.2 = f32[2,768,128]{2,0,1:T(2,128)S(1)} async-done(((f32[2,768,128]{2,0,1:T(2,128)}), f32[2,768,128]{2,0,1:T(2,128)S(1)}, u32[]{:S(2)}, u32[]{:S(2)}) %all-to-all-start.2) | async-done | bytes 786464 | tf_op jit(solution)/shard_map/all_to_all | solution.py:18
  100.0 0.1 copy.29
  100.0 0.0 copy-start.2
  100.1 0.6 copy.30
  100.7 0.4 fusion.32
  101.1 0.9 copy.31
  101.9 5.4 %all-to-all-start.3 = ((f32[16,48,128]{2,1,0:T(8,128)}), f32[16,48,128]{2,1,0:T(8,128)S(1)}, u32[]{:S(2)}, u32[]{:S(2)}) async-start(f32[16,48,128]{2,1,0:T(8,128)} %copy.31), calls=%async_computation.3 | async-start | bytes 786432 | tf_op jit(solution)/shard_map/all_to_all | solution.py:23
  107.4 0.0 copy-done.2
  107.4 0.2 copy.27
  107.5 12.0 %all-to-all-done.3 = f32[16,48,128]{2,1,0:T(8,128)S(1)} async-done(((f32[16,48,128]{2,1,0:T(8,128)}), f32[16,48,128]{2,1,0:T(8,128)S(1)}, u32[]{:S(2)}, u32[]{:S(2)}) %all-to-all-start.3) | async-done | bytes 393248 | tf_op jit(solution)/shard_map/all_to_all | solution.py:23
  119.6 3.7 %fusion.6 = f32[128,768]{0,1:T(8,128)S(1)} fusion(f32[3,768,768]{2,1,0:T(8,128)} %param.6, f32[1,768,128]{2,1,0:T(8,128)S(1)} %bitcast_subtract_fusion), kind=kOutput, calls=%fused_computation.6 | convolution fusion | flops 905969664 | bytes 3145728 | tf_op jit(solution)/shard_map/dot_general | solution.py:33
  123.3 0.3 convolution_bitcast_fusion
  123.6 32.0 %psum.7 = f32[128]{0:T(128)} all-reduce(f32[128]{0:T(128)S(1)} %convolution_bitcast_fusion), channel_id=1, replica_groups=mesh['parts'=2,'rows'=16] {'rows'}, use_global_device_ids=true, to_apply=%region_0.0 | all-reduce | flops 128 | bytes 1024 | tf_op jit(solution)/shard_map/psum | solution.py:50
  155.6 1.1 pad_maximum_fusion
  (3 shorter events, 0.1 us)
Async XLA Ops:
  11.7 8.7 %copy-start.3 = (s32[2,1,2]{2,1,0:T(1,128)S(1)}, s32[2,1,2]{2,1,0:T(1,128)}, u32[]{:S(2)}) copy-start(s32[2,1,2]{2,1,0:T(1,128)} %param.8) | copy-start | bytes 52
  12.9 54.8 %copy-start.1 = (f32[3,768,128]{2,1,0:T(8,128)S(1)}, f32[3,768,128]{2,1,0:T(8,128)}, u32[]{:S(2)}) copy-start(f32[3,768,128]{2,1,0:T(8,128)} %param.5) | copy-start | bytes 3538948
  12.9 36.8 %all-to-all-start = ((f32[2,768,128]{2,0,1:T(2,128)}), f32[2,768,128]{2,0,1:T(2,128)S(1)}, u32[]{:S(2)}, u32[]{:S(2)}) async-start(f32[2,768,128]{2,0,1:T(2,128)} %copy.23), calls=%async_computation | async-start | bytes 1572864 | tf_op jit(solution)/shard_map/all_to_all | solution.py:18
  49.7 21.8 %copy-start = (f32[2,2,768,768]{3,2,1,0:T(8,128)S(1)}, f32[2,2,768,768]{3,2,1,0:T(8,128)}, u32[]{:S(2)}) copy-start(f32[2,2,768,768]{3,2,1,0:T(8,128)} %param.7) | copy-start | bytes 28311556
  77.7 22.3 %all-to-all-start.2 = ((f32[2,768,128]{2,0,1:T(2,128)}), f32[2,768,128]{2,0,1:T(2,128)S(1)}, u32[]{:S(2)}, u32[]{:S(2)}) async-start(f32[2,768,128]{2,0,1:T(2,128)} %copy.28), calls=%async_computation.2 | async-start | bytes 1572864 | tf_op jit(solution)/shard_map/all_to_all | solution.py:18
  100.0 7.3 %copy-start.2 = (f32[768]{0:T(1024)S(1)}, f32[768]{0:T(1024)}, u32[]{:S(2)}) copy-start(f32[768]{0:T(1024)} %param.9) | copy-start | bytes 9220
  101.9 17.6 %all-to-all-start.3 = ((f32[16,48,128]{2,1,0:T(8,128)}), f32[16,48,128]{2,1,0:T(8,128)S(1)}, u32[]{:S(2)}, u32[]{:S(2)}) async-start(f32[16,48,128]{2,1,0:T(8,128)} %copy.31), calls=%async_computation.3 | async-start | bytes 786432 | tf_op jit(solution)/shard_map/all_to_all | solution.py:23
where the time goes:
time: 157 us
  blocking collectives  77.9 us (50%)
  waiting for transfers between devices  30.6 us (19%)
  matrix products  24.5 us (16%)
  starting transfers between devices  16.6 us (11%)
  local copies, waits for them, and re-layouts  5.05 us (3%)
    psum x1, blocking collectives, body(): observed = lax.psum(partial_sum, 'rows')  32 us
    all_gather x1, blocking collectives, body(): pattern = lax.all_gather(dest, 'rows', axis=1, tiled=True)  29.2 us
    all_to_all x2, waiting for transfers between devices, collect_updates(): lax.all_to_all(products, 'rows', split_axis=1, concat_axis=0, tiled=True)  18.6 us
    all_to_all x1, blocking collectives, collect_updates(): lax.all_to_all(partial_value, 'rows', split_axis=0, concat_axis=0, tiled=...  16.8 us
    dot_general x2, matrix products, collect_updates(): jnp.einsum('kab,bc->kac', tiles_level, solved_block, precision=lax.Precis...  12.3 us
    all_to_all x1, waiting for transfers between devices, collect_updates(): lax.all_to_all(partial_value, 'rows', split_axis=0, concat_axis=0, tiled=...  12 us
    all_to_all x2, starting transfers between devices, collect_updates(): lax.all_to_all(products, 'rows', split_axis=1, concat_axis=0, tiled=True)  11.1 us
    dot_general x3, matrix products, body(): jnp.dot(diag_inv[section], current, precision=lax.Precision.HIGHEST, pref...  11.1 us
  transfers between devices with their start and end apart: 3, of which 2 were waited for; matrix products, arithmetic and copies ran while one was open for 0% of the time, Pallas kernels for 0%

commit v1 on v0

v1 whole, which is shorter than its diff:
```python
import functools
import jax
import jax.numpy as jnp
from jax import lax
from jax.experimental import pallas as pl
from jax.experimental.pallas import tpu as pltpu
from jax.sharding import PartitionSpec as P

CAP = 4
PIECES = 4


def split(value):
    high = value.astype(jnp.bfloat16)
    return high, (value - high.astype(jnp.float32)).astype(jnp.bfloat16)


def dot_pair(high, low, right, width):
    wide = jnp.dot(high, right, preferred_element_type=jnp.float32)
    return (
        wide[:, :width]
        + wide[:, width:]
        + jnp.dot(low, right[:, :width], preferred_element_type=jnp.float32)
    )


def kernel(n, rhs, weight, dest, diag, tiles, sol, observed, *scratch):
    stage1 = [scratch[t * PIECES : (t + 1) * PIECES] for t in range(2)]
    (
        diag_f, tile_f, diag_hi, diag_lo, tile_hi, tile_lo, solved,
        send1, send2, recv2, own, send3, update, names, names_s, table, share, shares,
        load_sem, s1_send, s1_recv, s2_send, s2_recv, s3_send, s3_recv,
        n_send, n_recv, n_copy, o_send, o_recv,
    ) = scratch[2 * PIECES :]
    size, width = rhs.shape[1], rhs.shape[2]
    half, hubs = n // 2, n // 4
    block = size // PIECES
    rows = block // hubs
    me = lax.axis_index("rows")
    side = me // half
    base = side * half
    pos = me - base
    first_hub = (1 - side) * hubs
    is_hub = jnp.logical_and(pos >= first_hub, pos < first_hub + hubs)
    hub = pos - first_hub
    opposite = (1 - side) * half
    peer = me + hubs * (1 - 2 * side)

    barrier = pltpu.get_barrier_semaphore()
    for other in range(n):
        @pl.when(other != me)
        def _():
            pl.semaphore_signal(barrier, inc=1, device_id={"rows": other})

    loads = [pltpu.make_async_copy(diag.at[0], diag_f.at[0], load_sem.at[0])]
    loads += [pltpu.make_async_copy(tiles.at[0, k], tile_f.at[0, k], load_sem.at[1 + k]) for k in range(2)]
    loads += [pltpu.make_async_copy(diag.at[1], diag_f.at[1], load_sem.at[3])]
    loads += [pltpu.make_async_copy(tiles.at[1, k], tile_f.at[1, k], load_sem.at[4 + k]) for k in range(2)]
    loads += [pltpu.make_async_copy(diag.at[2], diag_f.at[2], load_sem.at[6])]
    for copy in loads:
        copy.start()

    strip = size // 8

    def split_into(source, high_ref, low_ref):
        def step(i, carry):
            at = pl.ds(pl.multiple_of(i * strip, strip), strip)
            high, low = split(source[at, :])
            high_ref[at, :] = high
            low_ref[at, :] = low
            return carry
        lax.fori_loop(0, 8, step, 0)

    def ready_diag(level):
        loads[3 * level].wait()
        split_into(diag_f.at[level], diag_hi.at[level], diag_lo.at[level])

    def ready_tiles(t):
        for k in range(2):
            loads[3 * t + 1 + k].wait()
            split_into(tile_f.at[t, k], tile_hi.at[t, k], tile_lo.at[t, k])

    def solve(level, current):
        high, low = split(current)
        right = jnp.concatenate([high, low], axis=1)
        solved[...] = right

        def step(i, carry):
            at = pl.ds(pl.multiple_of(i * block, block), block)
            sol[level, at, :] = dot_pair(diag_hi[level, at, :], diag_lo[level, at, :], solved[...], width)
            return carry
        lax.fori_loop(0, PIECES, step, 0)
        high, low = split(sol[level])
        solved[:, :width] = high
        solved[:, width:] = low

    def names_copy(p, slot):
        return pltpu.make_async_remote_copy(
            src_ref=share, dst_ref=names.at[slot], send_sem=n_send.at[p], recv_sem=n_recv.at[slot],
            device_id={"rows": base + first_hub + p})

    def first(t, c, p, slot):
        return pltpu.make_async_remote_copy(
            src_ref=send1.at[t, c, :, pl.ds(p * rows, rows), :],
            dst_ref=stage1[t][c].at[pl.ds(2 * slot, 2)],
            send_sem=s1_send.at[t, c, p], recv_sem=s1_recv.at[t, c, slot],
            device_id={"rows": base + first_hub + p})

    def second(t, c):
        return pltpu.make_async_remote_copy(
            src_ref=send2.at[t, c], dst_ref=recv2.at[t, c],
            send_sem=s2_send.at[t, c], recv_sem=s2_recv.at[t, c], device_id={"rows": peer})

    def third(t, c, owner, slot):
        at = pl.ds(c * block + slot * rows, rows)
        return pltpu.make_async_remote_copy(
            src_ref=send3.at[t, c, owner], dst_ref=update.at[t, at, :],
            send_sem=s3_send.at[t, c, owner], recv_sem=s3_recv.at[t, c, slot],
            device_id={"rows": base + owner})

    line = lax.broadcasted_iota(jnp.int32, share.shape, 0)
    lane = lax.broadcasted_iota(jnp.int32, share.shape, 1)
    value = jnp.zeros(share.shape, jnp.int32)
    for t in range(2):
        for k in range(2):
            value = jnp.where(jnp.logical_and(line == t, lane == k), dest[t, k], value)
    share[...] = value

    ready_diag(0)
    solve(0, rhs[0])
    ready_tiles(0)
    pl.semaphore_wait(barrier, n - 1)

    for p in range(hubs):
        mine = jnp.logical_and(is_hub, hub == p)

        @pl.when(jnp.logical_not(mine))
        def _():
            names_copy(p, pos).start()

        @pl.when(mine)
        def _():
            names[pos] = share[...]

    def build_table():
        for slot in range(half):
            @pl.when(slot != pos)
            def _():
                names_copy(0, slot).wait_recv()
        move = pltpu.make_async_copy(names, names_s, n_copy)
        move.start()
        move.wait()
        for t in range(2):
            def one(d, carry):
                count = jnp.int32(0)
                places = [jnp.int32(n)] * CAP
                for q in range(n):
                    hit = names_s[q // 2, t, q % 2] == d
                    for r in range(CAP):
                        places[r] = jnp.where(jnp.logical_and(hit, count == r), q, places[r])
                    count = count + jnp.where(hit, 1, 0)
                for r in range(CAP):
                    table[t, d * CAP + r] = places[r]
                return carry
            lax.fori_loop(0, n, one, 0)

    def add_up(t, c, start, out):
        buffer = stage1[t][c]

        def one(i, carry):
            at = (start + i) * CAP
            total = buffer[table[t, at]] + buffer[table[t, at + 1]]
            out[i] = total + (buffer[table[t, at + 2]] + buffer[table[t, at + 3]])
            return carry
        lax.fori_loop(0, half, one, 0)

    for t in range(2):
        for c in range(PIECES):
            for k in range(2):
                at = pl.ds(c * block, block)
                send1[t, c, k] = dot_pair(tile_hi[t, k, at, :], tile_lo[t, k, at, :], solved[...], width)
            for p in range(hubs):
                mine = jnp.logical_and(is_hub, hub == p)

                @pl.when(jnp.logical_not(mine))
                def _():
                    first(t, c, p, pos).start()

                @pl.when(mine)
                def _():
                    stage1[t][c][pl.ds(2 * pos, 2)] = send1[t, c, :, p * rows : (p + 1) * rows, :]
        ready_diag(t + 1)
        if t == 0:
            ready_tiles(1)

        @pl.when(is_hub)
        def _():
            if t == 0:
                build_table()

            def finish(c):
                second(t, c).wait_recv()

                def one(i, carry):
                    send3[t, c, i] = own[c % 2, i] + recv2[t, c, i]
                    return carry
                lax.fori_loop(0, half, one, 0)
                for owner in range(half):
                    @pl.when(owner != pos)
                    def _():
                        third(t, c, owner, hub).start()
                update[t, pl.ds(c * block + hub * rows, rows), :] = send3[t, c, pos]

            for c in range(PIECES):
                stage1[t][c][n] = jnp.zeros((rows, width), jnp.float32)
                for slot in range(half):
                    @pl.when(slot != pos)
                    def _():
                        first(t, c, 0, slot).wait_recv()
                add_up(t, c, opposite, send2.at[t, c])
                second(t, c).start()
                add_up(t, c, base, own.at[c % 2])
                if c > 0:
                    finish(c - 1)
            finish(PIECES - 1)

        for c in range(PIECES):
            for p in range(hubs):
                @pl.when(jnp.logical_not(jnp.logical_and(is_hub, hub == p)))
                def _():
                    third(t, c, 0, p).wait_recv()
        solve(t + 1, rhs[t + 1] - update[t])

    high, low = split(jnp.broadcast_to(weight[...], (16, size)))
    part = dot_pair(high, low, solved[...], width)
    shares[me] = part[:8]

    def total_copy(other, slot):
        return pltpu.make_async_remote_copy(
            src_ref=shares.at[me], dst_ref=shares.at[me], send_sem=o_send.at[other], recv_sem=o_recv.at[slot],
            device_id={"rows": other})

    for other in range(n):
        @pl.when(other != me)
        def _():
            total_copy(other, me).start()

    for p in range(hubs):
        @pl.when(jnp.logical_not(jnp.logical_and(is_hub, hub == p)))
        def _():
            names_copy(p, pos).wait_send()
            for t in range(2):
                for c in range(PIECES):
                    first(t, c, p, pos).wait_send()

    @pl.when(is_hub)
    def _():
        for t in range(2):
            for c in range(PIECES):
                second(t, c).wait_send()
                for owner in range(half):
                    @pl.when(owner != pos)
                    def _():
                        third(t, c, owner, hub).wait_send()

    for other in range(n):
        @pl.when(other != me)
        def _():
            pltpu.make_async_remote_copy(
                src_ref=shares.at[other], dst_ref=shares.at[other], send_sem=o_send.at[other],
                recv_sem=o_recv.at[other], device_id={"rows": other}).wait()
    total = shares[0]
    for other in range(1, n):
        total = total + shares[other]
    observed[...] = total[:1]


def body(rhs, diag_inv, tiles, dest, obs_weight):
    n = lax.axis_size("rows")
    size, width = rhs.shape[1], rhs.shape[2]
    half, hubs = n // 2, n // 4
    rows = size // PIECES // hubs
    f32, bf16 = jnp.float32, jnp.bfloat16
    dma = pltpu.SemaphoreType.DMA
    vmem = pl.BlockSpec(memory_space=pltpu.VMEM)
    anywhere = pl.BlockSpec(memory_space=pl.ANY)
    sol, observed = pl.pallas_call(
        functools.partial(kernel, n),
        out_shape=(
            jax.ShapeDtypeStruct((3, size, width), f32),
            jax.ShapeDtypeStruct((1, width), f32),
        ),
        in_specs=[vmem, vmem, pl.BlockSpec(memory_space=pltpu.SMEM), anywhere, anywhere],
        out_specs=(vmem, vmem),
        scratch_shapes=[pltpu.VMEM((n + 1, rows, width), f32) for _ in range(2 * PIECES)] + [
            pltpu.VMEM((3, size, size), f32),
            pltpu.VMEM((2, 2, size, size), f32),
            pltpu.VMEM((3, size, size), bf16),
            pltpu.VMEM((3, size, size), bf16),
            pltpu.VMEM((2, 2, size, size), bf16),
            pltpu.VMEM((2, 2, size, size), bf16),
            pltpu.VMEM((size, 2 * width), bf16),
            pltpu.VMEM((2, PIECES, 2, size // PIECES, width), f32),
            pltpu.VMEM((2, PIECES, half, rows, width), f32),
            pltpu.VMEM((2, PIECES, half, rows, width), f32),
            pltpu.VMEM((2, half, rows, width), f32),
            pltpu.VMEM((2, PIECES, half, rows, width), f32),
            pltpu.VMEM((2, size, width), f32),
            pltpu.VMEM((half, 8, 128), jnp.int32),
            pltpu.SMEM((half, 8, 128), jnp.int32),
            pltpu.SMEM((2, n * CAP), jnp.int32),
            pltpu.VMEM((8, 128), jnp.int32),
            pltpu.VMEM((n, 8, width), f32),
            dma((7,)),
            dma((2, PIECES, hubs)), dma((2, PIECES, half)),
            dma((2, PIECES)), dma((2, PIECES)),
            dma((2, PIECES, half)), dma((2, PIECES, hubs)),
            dma((hubs,)), dma((half,)), dma,
            dma((n,)), dma((n,)),
        ],
        compiler_params=pltpu.CompilerParams(
            collective_id=0, has_side_effects=True, vmem_limit_bytes=56 * 1024 * 1024
        ),
        cost_estimate=pl.CostEstimate(
            flops=7 * 3 * 2 * size * size * width, bytes_accessed=7 * 4 * size * size, transcendentals=0
        ),
    )(rhs, obs_weight.reshape(1, size), dest.reshape(2, 2), diag_inv, tiles)
    return sol, observed.reshape(width)


def solution(mesh):
    in_specs = (
        P(None, "rows", "parts"),
        P(None, "rows", None),
        P(None, "rows", None, None),
        P(None, "rows", None),
        P("rows"),
    )
    out_specs = (P(None, "rows", "parts"), P("parts"))
    return jax.shard_map(body, mesh=mesh, in_specs=in_specs, out_specs=out_specs, check_vma=False)
```

time: 157 us -> 84.7 us (0.54)
  Pallas kernels: 0 us -> 79.7 us
  blocking collectives: 77.9 us -> 0 us
  waiting for transfers between devices: 30.6 us -> 0 us
  matrix products: 24.5 us -> 0 us
  starting transfers between devices: 16.6 us -> 0 us
    pallas_call x0 -> x1, Pallas kernels: none -> 79.7 us  [body(): pl.pallas_call(functools.partial(kernel, n), out_shape=(jax.ShapeDtypeStr...]
    psum x1 -> x0, blocking collectives: 32 us -> none  [body(): observed = lax.psum(partial_sum, 'rows')]
    all_to_all x3 -> x0, waiting for transfers between devices: 30.6 us -> none  [the longest x2 18.6 us: collect_updates(): lax.all_to_all(products, 'rows', split_axis=1, concat_axis=0, tiled=True)]
    all_gather x1 -> x0, blocking collectives: 29.2 us -> none  [body(): pattern = lax.all_gather(dest, 'rows', axis=1, tiled=True)]
    dot_general x8 -> x0, matrix products: 24.5 us -> none  [the longest x2 12.3 us: collect_updates(): jnp.einsum('kab,bc->kac', tiles_level, solved_block, precision=lax.Precis...]
    all_to_all x1 -> x0, blocking collectives: 16.8 us -> none  [collect_updates(): lax.all_to_all(partial_value, 'rows', split_axis=0, concat_axis=0, tiled=...]
    all_to_all x3 -> x0, starting transfers between devices: 16.6 us -> none  [the longest x2 11.1 us: collect_updates(): lax.all_to_all(products, 'rows', split_axis=1, concat_axis=0, tiled=True)]
    dot_general x5 -> x0, local copies, waits for them, and re-layouts: 3.48 us -> none  [the longest x2 2.33 us: collect_updates(): jnp.einsum('kab,bc->kac', tiles_level, solved_block, precision=lax.Precis...]
  transfers between devices with their start and end apart: 3 -> 0, of which waited for: 2 -> 0; matrix products, arithmetic and copies ran while one was open for 0% -> 0% of each run, Pallas kernels for 0% -> 0%
where the time goes in v1:
time: 84.7 us; the launch traced here: 84.5 us
  Pallas kernels  79.7 us (94%)
  local copies, waits for them, and re-layouts  4.14 us (5%)
    pallas_call x1, Pallas kernels, body(): pl.pallas_call(functools.partial(kernel, n), out_shape=(jax.ShapeDtypeStr...  79.7 us
    unnamed x4, local copies, waits for them, and re-layouts  2.88 us

profile of v1, /device:TPU:0, one launch (start us, length us, event | category | flops | bytes accessed | tf_op | source)
XLA Modules:
  0.0 84.5 jit_solution(2076882261088397821)
XLA Ops:
  0.6 1.3 %reshape.13.weight = f32[1,768]{1,0:T(1,128)} reshape(f32[768]{0:T(1024)} %param.9) | data formatting | bytes 6144 | tf_op jit(solution)/shard_map/reshape | solution.py:327
  1.9 79.7 %shard_map.68 = (f32[3,768,128]{2,1,0:T(8,128)}, f32[1,128]{1,0:T(1,128)}) custom-call(f32[3,768,128]{2,1,0:T(8,128)} %rhs.1, f32[1,768]{1,0:T(1,128)} %reshape.13.weight, s32[2,2]{1,0:T(2,128)} %bitcast.2, f32[3,768,768]{2,1,0:T(8,128)} %diag.1, f32[2,2,768,768]{3,2,1,0:T(8,128)} %tiles.1), custom_call_target="tpu_custom_call" | custom-call | flops 3170893824 | bytes 16515072 | tf_op jit(solution)/shard_map/pallas_call | solution.py:287
  81.6 0.0 copy-start
  81.6 2.4 %copy.9 = f32[3,768,128]{2,1,0:T(8,128)} copy(f32[3,768,128]{2,1,0:T(8,128)} %get-tuple-element.8) | data formatting | bytes 2359296
  84.0 0.0 copy-done
  84.0 0.5 copy.10
Async XLA Ops:
  81.6 2.4 %copy-start = (f32[1,128]{1,0:T(1,128)S(1)}, f32[1,128]{1,0:T(1,128)}, u32[]{:S(2)}) copy-start(f32[1,128]{1,0:T(1,128)} %get-tuple-element.5) | copy-start | bytes 1540

commit v2 on v0

v2 whole, which is shorter than its diff:
```python
import functools
import jax
import jax.numpy as jnp
from jax import lax
from jax.experimental import pallas as pl
from jax.experimental.pallas import tpu as pltpu
from jax.sharding import PartitionSpec as P

CAP = 4
PIECES = 3


def split(value):
    high = value.astype(jnp.bfloat16)
    return high, (value - high.astype(jnp.float32)).astype(jnp.bfloat16)


def kernel(n, pieces, rhs, weight, dest, diag, tiles, sol, observed, *scratch):
    stage1 = [scratch[p * pieces : (p + 1) * pieces] for p in range(4)]
    (
        rhs_v, diag_f, tile_f, diag_hi, diag_lo, tile_hi, tile_lo, solved, sol_v,
        send1, send2, recv2, own, send3, update, share, names, places_v, table, shares,
        load_sem, out_sem, s1_send, s1_recv, s2_send, s2_recv, s3_send, s3_recv,
        n_send, n_recv, n_copy, o_send, o_recv,
    ) = scratch[4 * pieces :]
    size, width = rhs.shape[1], rhs.shape[2]
    half, hubs = n // 2, n // 4
    block = size // pieces
    packed = block // 2
    rows = packed // hubs
    me = lax.axis_index("rows")
    side = me // half
    base = side * half
    pos = me - base
    first_hub = (1 - side) * hubs
    is_hub = jnp.logical_and(pos >= first_hub, pos < first_hub + hubs)
    hub = pos - first_hub
    opposite = (1 - side) * half
    peer = me + hubs * (1 - 2 * side)

    barrier = pltpu.get_barrier_semaphore()
    for other in range(n):
        @pl.when(other != me)
        def _():
            pl.semaphore_signal(barrier, inc=1, device_id={"rows": other})

    loads = []

    def load(source, target):
        loads.append(pltpu.make_async_copy(source, target, load_sem.at[len(loads)]))
        loads[-1].start()

    for level in range(3):
        load(rhs.at[level], rhs_v.at[level])
        load(diag.at[level], diag_f.at[level])
        if level < 2:
            for k in range(2):
                load(tiles.at[level, k], tile_f.at[level, k])

    strip = size // 8

    def split_into(source, high_ref, low_ref):
        def step(i, carry):
            at = pl.ds(pl.multiple_of(i * strip, strip), strip)
            high, low = split(source[at, :])
            high_ref[at, :] = high
            low_ref[at, :] = low
            return carry
        lax.fori_loop(0, 8, step, 0)

    def ready_diag(level):
        loads[4 * level].wait()
        loads[4 * level + 1].wait()
        split_into(diag_f.at[level], diag_hi.at[level], diag_lo.at[level])

    def ready_tiles(level):
        for k in range(2):
            loads[4 * level + 2 + k].wait()
            split_into(tile_f.at[level, k], tile_hi.at[level, k], tile_lo.at[level, k])

    def left(shape):
        return lax.broadcasted_iota(jnp.int32, shape, 1) < width // 2

    def swap(value):
        return pltpu.roll(value, width // 2, 1)

    def twice(value, h):
        low, high = (value, swap(value)) if h == 0 else (swap(value), value)
        return jnp.where(left(value.shape), low, high)

    def keep(h, value):
        high, low = split(value)
        mask = left(value.shape)
        both = jnp.where(mask, high.astype(jnp.float32), low.astype(jnp.float32))
        solved[h, :, :width] = both.astype(jnp.bfloat16)
        solved[h, :, width:] = high

    def multiply(high, low, h):
        wide = jnp.dot(high, solved[h, :, :width], preferred_element_type=jnp.float32)
        return wide + swap(wide) + jnp.dot(low, solved[h, :, width:], preferred_element_type=jnp.float32)

    def solve(level, h, current):
        keep(h, current)
        for c in range(pieces):
            at = pl.ds(c * block, block)
            sol_v[h, at, :] = multiply(diag_hi[level, at, :], diag_lo[level, at, :], h)
        value = sol_v[h]
        keep(h, value)
        if h == 0:
            mixed = jnp.where(left(value.shape), value, rhs_v[level])
        else:
            mixed = jnp.where(left(value.shape), rhs_v[level], value)
        rhs_v[level] = mixed

    def result_copy(level):
        return pltpu.make_async_copy(rhs_v.at[level], sol.at[level], out_sem.at[level])

    def names_copy(p, slot):
        return pltpu.make_async_remote_copy(
            src_ref=share, dst_ref=names.at[slot], send_sem=n_send.at[p], recv_sem=n_recv.at[slot],
            device_id={"rows": base + first_hub + p})

    def first(p, c, to, slot):
        return pltpu.make_async_remote_copy(
            src_ref=send1.at[p, c, :, pl.ds(to * rows, rows), :],
            dst_ref=stage1[p][c].at[pl.ds(2 * slot, 2)],
            send_sem=s1_send.at[p, c, to], recv_sem=s1_recv.at[p, c, slot],
            device_id={"rows": base + first_hub + to})

    def second(p, c):
        return pltpu.make_async_remote_copy(
            src_ref=send2.at[p, c], dst_ref=recv2.at[p, c],
            send_sem=s2_send.at[p, c], recv_sem=s2_recv.at[p, c], device_id={"rows": peer})

    def third(p, c, owner, slot):
        return pltpu.make_async_remote_copy(
            src_ref=send3.at[p, c, owner], dst_ref=update.at[p, c, pl.ds(slot * rows, rows), :],
            send_sem=s3_send.at[p, c, owner], recv_sem=s3_recv.at[p, c, slot],
            device_id={"rows": base + owner})

    def send_products(p):
        t, h = p // 2, p % 2
        for c in range(pieces):
            at = pl.ds(c * block, block)
            for k in range(2):
                value = multiply(tile_hi[t, k, at, :], tile_lo[t, k, at, :], h)
                top, bottom = value[:packed], value[packed:]
                send1[p, c, k] = jnp.where(left(top.shape), top, bottom)
            for to in range(hubs):
                mine = jnp.logical_and(is_hub, hub == to)

                @pl.when(jnp.logical_not(mine))
                def _():
                    first(p, c, to, pos).start()

                @pl.when(mine)
                def _():
                    stage1[p][c][pl.ds(2 * pos, 2)] = send1[p, c, :, to * rows : (to + 1) * rows, :]

    def build_table():
        for slot in range(half):
            @pl.when(slot != pos)
            def _():
                names_copy(0, slot).wait_recv()
        shape = places_v.shape
        target = lax.broadcasted_iota(jnp.int32, shape, 0)
        turn = lax.broadcasted_iota(jnp.int32, shape, 1) % CAP
        count = jnp.zeros(shape, jnp.int32)
        place = jnp.full(shape, n, jnp.int32)
        for q in range(n):
            hit = jnp.broadcast_to(names[q // 2, q % 2 : q % 2 + 1, :], shape) == target
            place = jnp.where(jnp.logical_and(hit, count == turn), q, place)
            count = count + jnp.where(hit, 1, 0)
        places_v[...] = place
        move = pltpu.make_async_copy(places_v, table, n_copy)
        move.start()
        move.wait()

    def add_up(p, c, start, out):
        buffer, column = stage1[p][c], p // 2 * CAP

        def one(i, carry):
            d = start + i
            total = buffer[table[d, column]] + buffer[table[d, column + 1]]
            out[i] = total + (buffer[table[d, column + 2]] + buffer[table[d, column + 3]])
            return carry
        lax.fori_loop(0, half, one, 0)

    def finish(step):
        p, c = step // pieces, step % pieces
        second(p, c).wait_recv()

        def one(i, carry):
            send3[p, c, i] = own[step % 2, i] + recv2[p, c, i]
            return carry
        lax.fori_loop(0, half, one, 0)
        for owner in range(half):
            @pl.when(owner != pos)
            def _():
                third(p, c, owner, hub).start()
        update[p, c, pl.ds(hub * rows, rows), :] = send3[p, c, pos]

    def hub_step(step):
        p, c = step // pieces, step % pieces

        @pl.when(is_hub)
        def _():
            if step == 0:
                build_table()
            if step < 4 * pieces:
                for slot in range(half):
                    @pl.when(slot != pos)
                    def _():
                        first(p, c, 0, slot).wait_recv()
                add_up(p, c, opposite, send2.at[p, c])
                second(p, c).start()
                add_up(p, c, base, own.at[step % 2])
            if step > 0:
                finish(step - 1)

    def receive(p):
        t, h = p // 2, p % 2
        for c in range(pieces):
            for slot in range(hubs):
                @pl.when(jnp.logical_not(jnp.logical_and(is_hub, hub == slot)))
                def _():
                    third(p, c, 0, slot).wait_recv()
        parts = []
        for c in range(pieces):
            value = update[p, c]
            parts += [twice(value, 0), twice(value, 1)]
        solve(t + 1, h, twice(rhs_v[t + 1], h) - jnp.concatenate(parts, axis=0))

    line = lax.broadcasted_iota(jnp.int32, share.shape, 0)
    lane = lax.broadcasted_iota(jnp.int32, share.shape, 1)
    value = jnp.zeros(share.shape, jnp.int32)
    for k in range(2):
        value = jnp.where(line == k, jnp.where(lane < CAP, dest[0, k], dest[1, k]), value)
    share[...] = value
    for p in range(4):
        for c in range(pieces):
            stage1[p][c][n] = jnp.zeros((rows, width), jnp.float32)

    ready_diag(0)
    solve(0, 0, twice(rhs_v[0], 0))
    pl.semaphore_wait(barrier, n - 1)
    for to in range(hubs):
        mine = jnp.logical_and(is_hub, hub == to)

        @pl.when(jnp.logical_not(mine))
        def _():
            names_copy(to, pos).start()

        @pl.when(mine)
        def _():
            names[pos] = share[...]
    ready_tiles(0)
    send_products(0)
    solve(0, 1, twice(rhs_v[0], 1))
    result_copy(0).start()
    send_products(1)

    for step in range(4 * pieces + 1):
        hub_step(step)
        if step == 0:
            ready_diag(1)
            ready_tiles(1)
        if step == 2 * pieces:
            ready_diag(2)
        if step == pieces + 1:
            receive(0)
            send_products(2)
        if step == 2 * pieces + 1:
            receive(1)
            result_copy(1).start()
            send_products(3)
        if step == 3 * pieces + 1:
            receive(2)
    receive(3)
    result_copy(2).start()

    high, low = split(jnp.broadcast_to(weight[...].reshape(1, size), (16, size)))
    part = [multiply(high, low, h)[:8] for h in range(2)]
    shares[me] = jnp.where(left(part[0].shape), part[0], part[1])

    for other in range(n):
        @pl.when(other != me)
        def _():
            pltpu.make_async_remote_copy(
                src_ref=shares.at[me], dst_ref=shares.at[me], send_sem=o_send.at[other],
                recv_sem=o_recv.at[me], device_id={"rows": other}).start()

    for to in range(hubs):
        @pl.when(jnp.logical_not(jnp.logical_and(is_hub, hub == to)))
        def _():
            names_copy(to, pos).wait_send()
            for p in range(4):
                for c in range(pieces):
                    first(p, c, to, pos).wait_send()

    @pl.when(is_hub)
    def _():
        for p in range(4):
            for c in range(pieces):
                second(p, c).wait_send()
                for owner in range(half):
                    @pl.when(owner != pos)
                    def _():
                        third(p, c, owner, hub).wait_send()

    for other in range(n):
        @pl.when(other != me)
        def _():
            pltpu.make_async_remote_copy(
                src_ref=shares.at[other], dst_ref=shares.at[other], send_sem=o_send.at[other],
                recv_sem=o_recv.at[other], device_id={"rows": other}).wait()
    total = shares[0]
    for other in range(1, n):
        total = total + shares[other]
    observed[...] = total[:1]
    for level in range(3):
        result_copy(level).wait()


def body(rhs, diag_inv, tiles, dest, obs_weight):
    n = lax.axis_size("rows")
    size, width = rhs.shape[1], rhs.shape[2]
    half, hubs = n // 2, n // 4
    pieces = PIECES
    packed = size // pieces // 2
    rows = packed // hubs
    f32, bf16 = jnp.float32, jnp.bfloat16
    dma = pltpu.SemaphoreType.DMA
    vmem = pl.BlockSpec(memory_space=pltpu.VMEM)
    anywhere = pl.BlockSpec(memory_space=pl.ANY)
    sol, observed = pl.pallas_call(
        functools.partial(kernel, n, pieces),
        out_shape=(
            jax.ShapeDtypeStruct((3, size, width), f32),
            jax.ShapeDtypeStruct((1, width), f32),
        ),
        in_specs=[anywhere, vmem, pl.BlockSpec(memory_space=pltpu.SMEM), anywhere, anywhere],
        out_specs=(anywhere, vmem),
        scratch_shapes=[pltpu.VMEM((n + 1, rows, width), f32) for _ in range(4 * pieces)] + [
            pltpu.VMEM((3, size, width), f32),
            pltpu.VMEM((3, size, size), f32),
            pltpu.VMEM((2, 2, size, size), f32),
            pltpu.VMEM((3, size, size), bf16),
            pltpu.VMEM((3, size, size), bf16),
            pltpu.VMEM((2, 2, size, size), bf16),
            pltpu.VMEM((2, 2, size, size), bf16),
            pltpu.VMEM((2, size, 2 * width), bf16),
            pltpu.VMEM((2, size, width), f32),
            pltpu.VMEM((4, pieces, 2, packed, width), f32),
            pltpu.VMEM((4, pieces, half, rows, width), f32),
            pltpu.VMEM((4, pieces, half, rows, width), f32),
            pltpu.VMEM((2, half, rows, width), f32),
            pltpu.VMEM((4, pieces, half, rows, width), f32),
            pltpu.VMEM((4, pieces, packed, width), f32),
            pltpu.VMEM((8, 128), jnp.int32),
            pltpu.VMEM((half, 8, 128), jnp.int32),
            pltpu.VMEM((n, 128), jnp.int32),
            pltpu.SMEM((n, 128), jnp.int32),
            pltpu.VMEM((n, 8, width), f32),
            dma((10,)), dma((3,)),
            dma((4, pieces, hubs)), dma((4, pieces, half)),
            dma((4, pieces)), dma((4, pieces)),
            dma((4, pieces, half)), dma((4, pieces, hubs)),
            dma((hubs,)), dma((half,)), dma,
            dma((n,)), dma((n,)),
        ],
        compiler_params=pltpu.CompilerParams(
            collective_id=0, has_side_effects=True, vmem_limit_bytes=60 * 1024 * 1024
        ),
        cost_estimate=pl.CostEstimate(
            flops=7 * 3 * 2 * size * size * width, bytes_accessed=7 * 4 * size * size, transcendentals=0
        ),
    )(rhs, obs_weight, dest.reshape(2, 2), diag_inv, tiles)
    return sol, observed.reshape(width)


def solution(mesh):
    in_specs = (
        P(None, "rows", "parts"),
        P(None, "rows", None),
        P(None, "rows", None, None),
        P(None, "rows", None),
        P("rows"),
    )
    out_specs = (P(None, "rows", "parts"), P("parts"))
    return jax.shard_map(body, mesh=mesh, in_specs=in_specs, out_specs=out_specs, check_vma=False)
```

time: 157 us -> 76.7 us (0.49)
  blocking collectives: 77.9 us -> 0 us
  Pallas kernels: 0 us -> 73 us
  waiting for transfers between devices: 30.6 us -> 0 us
  matrix products: 24.5 us -> 0 us
  starting transfers between devices: 16.6 us -> 0 us
  local copies, waits for them, and re-layouts: 5.05 us -> 2.88 us
    pallas_call x0 -> x1, Pallas kernels: none -> 73 us  [body(): pl.pallas_call(functools.partial(kernel, n, pieces), out_shape=(jax.Shape...]
    psum x1 -> x0, blocking collectives: 32 us -> none  [body(): observed = lax.psum(partial_sum, 'rows')]
    all_to_all x3 -> x0, waiting for transfers between devices: 30.6 us -> none  [the longest x2 18.6 us: collect_updates(): lax.all_to_all(products, 'rows', split_axis=1, concat_axis=0, tiled=True)]
    all_gather x1 -> x0, blocking collectives: 29.2 us -> none  [body(): pattern = lax.all_gather(dest, 'rows', axis=1, tiled=True)]
    dot_general x8 -> x0, matrix products: 24.5 us -> none  [the longest x2 12.3 us: collect_updates(): jnp.einsum('kab,bc->kac', tiles_level, solved_block, precision=lax.Precis...]
    all_to_all x1 -> x0, blocking collectives: 16.8 us -> none  [collect_updates(): lax.all_to_all(partial_value, 'rows', split_axis=0, concat_axis=0, tiled=...]
    all_to_all x3 -> x0, starting transfers between devices: 16.6 us -> none  [the longest x2 11.1 us: collect_updates(): lax.all_to_all(products, 'rows', split_axis=1, concat_axis=0, tiled=True)]
    dot_general x5 -> x0, local copies, waits for them, and re-layouts: 3.48 us -> none  [the longest x2 2.33 us: collect_updates(): jnp.einsum('kab,bc->kac', tiles_level, solved_block, precision=lax.Precis...]
  transfers between devices with their start and end apart: 3 -> 0, of which waited for: 2 -> 0; matrix products, arithmetic and copies ran while one was open for 0% -> 0% of each run, Pallas kernels for 0% -> 0%
where the time goes in v2:
time: 76.7 us; the launch traced here: 76.5 us
  Pallas kernels  73 us (95%)
  local copies, waits for them, and re-layouts  2.88 us (4%)
    pallas_call x1, Pallas kernels, body(): pl.pallas_call(functools.partial(kernel, n, pieces), out_shape=(jax.Shape...  73 us
    unnamed x4, local copies, waits for them, and re-layouts  2.88 us

profile of v2, /device:TPU:0, one launch (start us, length us, event | category | flops | bytes accessed | tf_op | source)
XLA Modules:
  0.0 76.5 jit_solution(11306834933750552806)
XLA Ops:
  0.6 73.0 %shard_map.68 = (f32[3,768,128]{2,1,0:T(8,128)}, f32[1,128]{1,0:T(1,128)}) custom-call(f32[3,768,128]{2,1,0:T(8,128)} %rhs.1, f32[768]{0:T(1024)} %weight.1, s32[2,2]{1,0:T(2,128)} %bitcast.2, f32[3,768,768]{2,1,0:T(8,128)} %diag.1, f32[2,2,768,768]{3,2,1,0:T(8,128)} %tiles.1), custom_call_target="tpu_custom_call" | custom-call | flops 3170893824 | bytes 16515072 | tf_op jit(solution)/shard_map/pallas_call | solution.py:336
  73.6 0.0 copy-start
  73.7 2.4 %copy.9 = f32[3,768,128]{2,1,0:T(8,128)} copy(f32[3,768,128]{2,1,0:T(8,128)} %get-tuple-element.8) | data formatting | bytes 2359296
  76.0 0.0 copy-done
  76.0 0.5 copy.10
Async XLA Ops:
  73.6 2.4 %copy-start = (f32[1,128]{1,0:T(1,128)S(1)}, f32[1,128]{1,0:T(1,128)}, u32[]{:S(2)}) copy-start(f32[1,128]{1,0:T(1,128)} %get-tuple-element.5) | copy-start | bytes 1540

commit v3 on v2

--- a/solution.py
+++ b/solution.py
@@ -39,16 +39,16 @@
     peer = me + hubs * (1 - 2 * side)
 
     barrier = pltpu.get_barrier_semaphore()
-    for other in range(n):
-        @pl.when(other != me)
-        def _():
-            pl.semaphore_signal(barrier, inc=1, device_id={"rows": other})
+    for j in range(1, n):
+        pl.semaphore_signal(barrier, inc=1, device_id={"rows": lax.rem(me + j, n)})
+
+    def await_bytes(ref, sem):
+        pltpu.make_async_copy(ref, ref, sem).wait()
 
     loads = []
 
     def load(source, target):
         loads.append(pltpu.make_async_copy(source, target, load_sem.at[len(loads)]))
-        loads[-1].start()
 
     for level in range(3):
         load(rhs.at[level], rhs_v.at[level])
@@ -56,6 +56,8 @@
         if level < 2:
             for k in range(2):
                 load(tiles.at[level, k], tile_f.at[level, k])
+    for copy in loads[:4]:
+        copy.start()
 
     strip = size // 8
 
@@ -115,16 +117,16 @@
     def result_copy(level):
         return pltpu.make_async_copy(rhs_v.at[level], sol.at[level], out_sem.at[level])
 
-    def names_copy(p, slot):
+    def names_copy(to):
         return pltpu.make_async_remote_copy(
-            src_ref=share, dst_ref=names.at[slot], send_sem=n_send.at[p], recv_sem=n_recv.at[slot],
-            device_id={"rows": base + first_hub + p})
-
-    def first(p, c, to, slot):
+            src_ref=share, dst_ref=names.at[pos], send_sem=n_send, recv_sem=n_recv,
+            device_id={"rows": base + first_hub + to})
+
+    def first(p, c, to):
         return pltpu.make_async_remote_copy(
-            src_ref=send1.at[p, c, :, pl.ds(to * rows, rows), :],
-            dst_ref=stage1[p][c].at[pl.ds(2 * slot, 2)],
-            send_sem=s1_send.at[p, c, to], recv_sem=s1_recv.at[p, c, slot],
+            src_ref=send1.at[p, c, :, pl.ds(pl.multiple_of(to * rows, rows), rows), :],
+            dst_ref=stage1[p][c].at[pl.ds(2 * pos, 2)],
+            send_sem=s1_send.at[p], recv_sem=s1_recv.at[p, c],
             device_id={"rows": base + first_hub + to})
 
     def second(p, c):
@@ -132,10 +134,11 @@
             src_ref=send2.at[p, c], dst_ref=recv2.at[p, c],
             send_sem=s2_send.at[p, c], recv_sem=s2_recv.at[p, c], device_id={"rows": peer})
 
-    def third(p, c, owner, slot):
+    def third(p, c, owner):
+        at = pl.ds(pl.multiple_of(hub * rows, rows), rows)
         return pltpu.make_async_remote_copy(
-            src_ref=send3.at[p, c, owner], dst_ref=update.at[p, c, pl.ds(slot * rows, rows), :],
-            send_sem=s3_send.at[p, c, owner], recv_sem=s3_recv.at[p, c, slot],
+            src_ref=send3.at[p, c, owner], dst_ref=update.at[p, c, at, :],
+            send_sem=s3_send.at[p], recv_sem=s3_recv.at[p],
             device_id={"rows": base + owner})
 
     def send_products(p):
@@ -146,22 +149,20 @@
                 value = multiply(tile_hi[t, k, at, :], tile_lo[t, k, at, :], h)
                 top, bottom = value[:packed], value[packed:]
                 send1[p, c, k] = jnp.where(left(top.shape), top, bottom)
-            for to in range(hubs):
-                mine = jnp.logical_and(is_hub, hub == to)
-
-                @pl.when(jnp.logical_not(mine))
-                def _():
-                    first(p, c, to, pos).start()
-
-                @pl.when(mine)
-                def _():
-                    stage1[p][c][pl.ds(2 * pos, 2)] = send1[p, c, :, to * rows : (to + 1) * rows, :]
+            @pl.when(is_hub)
+            def _():
+                at = pl.ds(pl.multiple_of(hub * rows, rows), rows)
+                stage1[p][c][pl.ds(2 * pos, 2)] = send1[p, c, :, at, :]
+
+            @pl.when(jnp.logical_not(is_hub))
+            def _():
+                first(p, c, lax.rem(pos, hubs)).start()
+
+            for j in range(1, hubs):
+                first(p, c, lax.rem(pos + j, hubs)).start()
 
     def build_table():
-        for slot in range(half):
-            @pl.when(slot != pos)
-            def _():
-                names_copy(0, slot).wait_recv()
+        await_bytes(names.at[pl.ds(0, half - 1)], n_recv)
         shape = places_v.shape
         target = lax.broadcasted_iota(jnp.int32, shape, 0)
         turn = lax.broadcasted_iota(jnp.int32, shape, 1) % CAP
@@ -179,26 +180,20 @@
     def add_up(p, c, start, out):
         buffer, column = stage1[p][c], p // 2 * CAP
 
-        def one(i, carry):
+        for i in range(half):
             d = start + i
             total = buffer[table[d, column]] + buffer[table[d, column + 1]]
             out[i] = total + (buffer[table[d, column + 2]] + buffer[table[d, column + 3]])
-            return carry
-        lax.fori_loop(0, half, one, 0)
 
     def finish(step):
         p, c = step // pieces, step % pieces
         second(p, c).wait_recv()
 
-        def one(i, carry):
+        for i in range(half):
             send3[p, c, i] = own[step % 2, i] + recv2[p, c, i]
-            return carry
-        lax.fori_loop(0, half, one, 0)
-        for owner in range(half):
-            @pl.when(owner != pos)
-            def _():
-                third(p, c, owner, hub).start()
-        update[p, c, pl.ds(hub * rows, rows), :] = send3[p, c, pos]
+        for j in range(1, half):
+            third(p, c, lax.rem(pos + j, half)).start()
+        update[p, c, pl.ds(pl.multiple_of(hub * rows, rows), rows), :] = send3[p, c, pos]
 
     def hub_step(step):
         p, c = step // pieces, step % pieces
@@ -208,10 +203,7 @@
             if step == 0:
                 build_table()
             if step < 4 * pieces:
-                for slot in range(half):
-                    @pl.when(slot != pos)
-                    def _():
-                        first(p, c, 0, slot).wait_recv()
+                await_bytes(stage1[p][c].at[pl.ds(0, 2 * (half - 1))], s1_recv.at[p, c])
                 add_up(p, c, opposite, send2.at[p, c])
                 second(p, c).start()
                 add_up(p, c, base, own.at[step % 2])
@@ -220,11 +212,14 @@
 
     def receive(p):
         t, h = p // 2, p % 2
-        for c in range(pieces):
-            for slot in range(hubs):
-                @pl.when(jnp.logical_not(jnp.logical_and(is_hub, hub == slot)))
-                def _():
-                    third(p, c, 0, slot).wait_recv()
+        @pl.when(is_hub)
+        def _():
+            await_bytes(update.at[p, :, pl.ds(0, packed - rows), :], s3_recv.at[p])
+
+        @pl.when(jnp.logical_not(is_hub))
+        def _():
+            await_bytes(update.at[p], s3_recv.at[p])
+
         parts = []
         for c in range(pieces):
             value = update[p, c]
@@ -244,17 +239,19 @@
     ready_diag(0)
     solve(0, 0, twice(rhs_v[0], 0))
     pl.semaphore_wait(barrier, n - 1)
-    for to in range(hubs):
-        mine = jnp.logical_and(is_hub, hub == to)
-
-        @pl.when(jnp.logical_not(mine))
-        def _():
-            names_copy(to, pos).start()
-
-        @pl.when(mine)
-        def _():
-            names[pos] = share[...]
+    @pl.when(is_hub)
+    def _():
+        names[pos] = share[...]
+
+    @pl.when(jnp.logical_not(is_hub))
+    def _():
+        names_copy(lax.rem(pos, hubs)).start()
+
+    for j in range(1, hubs):
+        names_copy(lax.rem(pos + j, hubs)).start()
     ready_tiles(0)
+    for copy in loads[4:]:
+        copy.start()
     send_products(0)
     solve(0, 1, twice(rhs_v[0], 1))
     result_copy(0).start()
@@ -283,37 +280,28 @@
     part = [multiply(high, low, h)[:8] for h in range(2)]
     shares[me] = jnp.where(left(part[0].shape), part[0], part[1])
 
-    for other in range(n):
-        @pl.when(other != me)
-        def _():
-            pltpu.make_async_remote_copy(
-                src_ref=shares.at[me], dst_ref=shares.at[me], send_sem=o_send.at[other],
-                recv_sem=o_recv.at[me], device_id={"rows": other}).start()
-
-    for to in range(hubs):
-        @pl.when(jnp.logical_not(jnp.logical_and(is_hub, hub == to)))
-        def _():
-            names_copy(to, pos).wait_send()
-            for p in range(4):
-                for c in range(pieces):
-                    first(p, c, to, pos).wait_send()
+    for j in range(1, n):
+        pltpu.make_async_remote_copy(
+            src_ref=shares.at[me], dst_ref=shares.at[me], send_sem=o_send,
+            recv_sem=o_recv, device_id={"rows": lax.rem(me + j, n)}).start()
 
     @pl.when(is_hub)
     def _():
+        await_bytes(names.at[pl.ds(0, hubs - 1)], n_send)
         for p in range(4):
+            await_bytes(send1.at[p, :, :, pl.ds(0, packed - rows), :], s1_send.at[p])
+            await_bytes(send3.at[p, :, pl.ds(0, half - 1)], s3_send.at[p])
             for c in range(pieces):
                 second(p, c).wait_send()
-                for owner in range(half):
-                    @pl.when(owner != pos)
-                    def _():
-                        third(p, c, owner, hub).wait_send()
-
-    for other in range(n):
-        @pl.when(other != me)
-        def _():
-            pltpu.make_async_remote_copy(
-                src_ref=shares.at[other], dst_ref=shares.at[other], send_sem=o_send.at[other],
-                recv_sem=o_recv.at[other], device_id={"rows": other}).wait()
+
+    @pl.when(jnp.logical_not(is_hub))
+    def _():
+        await_bytes(names.at[pl.ds(0, hubs)], n_send)
+        for p in range(4):
+            await_bytes(send1.at[p], s1_send.at[p])
+
+    await_bytes(shares.at[pl.ds(0, n - 1)], o_send)
+    await_bytes(shares.at[pl.ds(0, n - 1)], o_recv)
     total = shares[0]
     for other in range(1, n):
         total = total + shares[other]
@@ -363,11 +351,10 @@
             pltpu.SMEM((n, 128), jnp.int32),
             pltpu.VMEM((n, 8, width), f32),
             dma((10,)), dma((3,)),
-            dma((4, pieces, hubs)), dma((4, pieces, half)),
+            dma((4,)), dma((4, pieces)),
             dma((4, pieces)), dma((4, pieces)),
-            dma((4, pieces, half)), dma((4, pieces, hubs)),
-            dma((hubs,)), dma((half,)), dma,
-            dma((n,)), dma((n,)),
+            dma((4,)), dma((4,)),
+            dma, dma, dma, dma, dma,
         ],
         compiler_params=pltpu.CompilerParams(
             collective_id=0, has_side_effects=True, vmem_limit_bytes=60 * 1024 * 1024

time: 76.7 us -> 74.3 us (0.969)
  Pallas kernels: 73 us -> 70.5 us
    pallas_call x1, Pallas kernels: 73 us -> 70.5 us  [body(): pl.pallas_call(functools.partial(kernel, n, pieces), out_shape=(jax.Shape...]
where the time goes in v3:
time: 74.3 us; the launch traced here: 74.1 us
  Pallas kernels  70.5 us (95%)
  local copies, waits for them, and re-layouts  2.88 us (4%)
    pallas_call x1, Pallas kernels, body(): pl.pallas_call(functools.partial(kernel, n, pieces), out_shape=(jax.Shape...  70.5 us
    unnamed x4, local copies, waits for them, and re-layouts  2.88 us

profile of v3, /device:TPU:0, one launch (start us, length us, event | category | flops | bytes accessed | tf_op | source)
XLA Modules:
  0.0 74.1 jit_solution(15063449587003946393)
XLA Ops:
  0.6 70.5 %shard_map.68 = (f32[3,768,128]{2,1,0:T(8,128)}, f32[1,128]{1,0:T(1,128)}) custom-call(f32[3,768,128]{2,1,0:T(8,128)} %rhs.1, f32[768]{0:T(1024)} %weight.1, s32[2,2]{1,0:T(2,128)} %bitcast.2, f32[3,768,768]{2,1,0:T(8,128)} %diag.1, f32[2,2,768,768]{3,2,1,0:T(8,128)} %tiles.1), custom_call_target="tpu_custom_call" | custom-call | flops 3170893824 | bytes 16515072 | tf_op jit(solution)/shard_map/pallas_call | solution.py:324
  71.2 0.0 copy-start
  71.2 2.4 %copy.9 = f32[3,768,128]{2,1,0:T(8,128)} copy(f32[3,768,128]{2,1,0:T(8,128)} %get-tuple-element.8) | data formatting | bytes 2359296
  73.6 0.0 copy-done
  73.6 0.5 copy.10
Async XLA Ops:
  71.2 2.4 %copy-start = (f32[1,128]{1,0:T(1,128)S(1)}, f32[1,128]{1,0:T(1,128)}, u32[]{:S(2)}) copy-start(f32[1,128]{1,0:T(1,128)} %get-tuple-element.5) | copy-start | bytes 1540

commit v4 on v3

--- a/solution.py
+++ b/solution.py
@@ -1,4 +1,5 @@
 import functools
+import math
 import jax
 import jax.numpy as jnp
 from jax import lax
@@ -8,6 +9,7 @@
 
 CAP = 4
 PIECES = 3
+OWN = 4
 
 
 def split(value):
@@ -59,26 +61,31 @@
     for copy in loads[:4]:
         copy.start()
 
-    strip = size // 8
-
-    def split_into(source, high_ref, low_ref):
+    strip = math.gcd(block, 64)
+
+    def split_rows(source, high_ref, low_ref, start, count):
         def step(i, carry):
-            at = pl.ds(pl.multiple_of(i * strip, strip), strip)
+            at = pl.ds(pl.multiple_of(start + i * strip, strip), strip)
             high, low = split(source[at, :])
             high_ref[at, :] = high
             low_ref[at, :] = low
             return carry
-        lax.fori_loop(0, 8, step, 0)
-
-    def ready_diag(level):
+        lax.fori_loop(0, count // strip, step, 0)
+
+    def await_diag(level):
         loads[4 * level].wait()
         loads[4 * level + 1].wait()
-        split_into(diag_f.at[level], diag_hi.at[level], diag_lo.at[level])
-
-    def ready_tiles(level):
+
+    def split_diag(level, start, count):
+        split_rows(diag_f.at[level], diag_hi.at[level], diag_lo.at[level], start, count)
+
+    def await_tiles(level):
         for k in range(2):
             loads[4 * level + 2 + k].wait()
-            split_into(tile_f.at[level, k], tile_hi.at[level, k], tile_lo.at[level, k])
+
+    def split_tiles(level, start, count):
+        for k in range(2):
+            split_rows(tile_f.at[level, k], tile_hi.at[level, k], tile_lo.at[level, k], start, count)
 
     def left(shape):
         return lax.broadcasted_iota(jnp.int32, shape, 1) < width // 2
@@ -144,6 +151,8 @@
     def send_products(p):
         t, h = p // 2, p % 2
         for c in range(pieces):
+            if p == 0:
+                split_tiles(0, c * block, block)
             at = pl.ds(c * block, block)
             for k in range(2):
                 value = multiply(tile_hi[t, k, at, :], tile_lo[t, k, at, :], h)
@@ -185,30 +194,32 @@
             total = buffer[table[d, column]] + buffer[table[d, column + 1]]
             out[i] = total + (buffer[table[d, column + 2]] + buffer[table[d, column + 3]])
 
+    def give_back(step):
+        @pl.when(is_hub)
+        def _():
+            finish(step)
+
     def finish(step):
         p, c = step // pieces, step % pieces
         second(p, c).wait_recv()
 
         for i in range(half):
-            send3[p, c, i] = own[step % 2, i] + recv2[p, c, i]
+            send3[p, c, i] = own[step % OWN, i] + recv2[p, c, i]
         for j in range(1, half):
             third(p, c, lax.rem(pos + j, half)).start()
         update[p, c, pl.ds(pl.multiple_of(hub * rows, rows), rows), :] = send3[p, c, pos]
 
-    def hub_step(step):
+    def gather(step):
         p, c = step // pieces, step % pieces
 
         @pl.when(is_hub)
         def _():
             if step == 0:
                 build_table()
-            if step < 4 * pieces:
-                await_bytes(stage1[p][c].at[pl.ds(0, 2 * (half - 1))], s1_recv.at[p, c])
-                add_up(p, c, opposite, send2.at[p, c])
-                second(p, c).start()
-                add_up(p, c, base, own.at[step % 2])
-            if step > 0:
-                finish(step - 1)
+            await_bytes(stage1[p][c].at[pl.ds(0, 2 * (half - 1))], s1_recv.at[p, c])
+            add_up(p, c, opposite, send2.at[p, c])
+            second(p, c).start()
+            add_up(p, c, base, own.at[step % OWN])
 
     def receive(p):
         t, h = p // 2, p % 2
@@ -236,7 +247,8 @@
         for c in range(pieces):
             stage1[p][c][n] = jnp.zeros((rows, width), jnp.float32)
 
-    ready_diag(0)
+    await_diag(0)
+    split_diag(0, 0, size)
     solve(0, 0, twice(rhs_v[0], 0))
     pl.semaphore_wait(barrier, n - 1)
     @pl.when(is_hub)
@@ -249,7 +261,7 @@
 
     for j in range(1, hubs):
         names_copy(lax.rem(pos + j, hubs)).start()
-    ready_tiles(0)
+    await_tiles(0)
     for copy in loads[4:]:
         copy.start()
     send_products(0)
@@ -257,22 +269,38 @@
     result_copy(0).start()
     send_products(1)
 
-    for step in range(4 * pieces + 1):
-        hub_step(step)
-        if step == 0:
-            ready_diag(1)
-            ready_tiles(1)
-        if step == 2 * pieces:
-            ready_diag(2)
-        if step == pieces + 1:
-            receive(0)
-            send_products(2)
-        if step == 2 * pieces + 1:
-            receive(1)
-            result_copy(1).start()
-            send_products(3)
-        if step == 3 * pieces + 1:
-            receive(2)
+    gather(0)
+    await_diag(1)
+    split_diag(1, 0, size)
+    await_tiles(1)
+    split_tiles(1, 0, size)
+    for step in range(1, pieces + 1):
+        gather(step)
+        give_back(step - 1)
+    for step in range(pieces + 1, 2 * pieces):
+        gather(step)
+        if step < 2 * pieces - 1:
+            give_back(step - 1)
+    receive(0)
+    send_products(2)
+    for step in range(2 * pieces - 2, 2 * pieces):
+        give_back(step)
+    await_diag(2)
+    split_diag(2, 0, size)
+    gather(2 * pieces)
+    receive(1)
+    result_copy(1).start()
+    send_products(3)
+    for step in range(2 * pieces + 1, 3 * pieces + 1):
+        gather(step)
+        give_back(step - 1)
+    for step in range(3 * pieces + 1, 4 * pieces):
+        gather(step)
+        if step < 4 * pieces - 1:
+            give_back(step - 1)
+    receive(2)
+    for step in range(4 * pieces - 2, 4 * pieces):
+        give_back(step)
     receive(3)
     result_copy(2).start()
 
@@ -342,7 +370,7 @@
             pltpu.VMEM((4, pieces, 2, packed, width), f32),
             pltpu.VMEM((4, pieces, half, rows, width), f32),
             pltpu.VMEM((4, pieces, half, rows, width), f32),
-            pltpu.VMEM((2, half, rows, width), f32),
+            pltpu.VMEM((OWN, half, rows, width), f32),
             pltpu.VMEM((4, pieces, half, rows, width), f32),
             pltpu.VMEM((4, pieces, packed, width), f32),
             pltpu.VMEM((8, 128), jnp.int32),

time: 74.3 us -> 74.9 us (level)
  no operation moved by 1% of the time
where the time goes in v4:
time: 74.9 us; the launch traced here: 74.7 us
  Pallas kernels  71.1 us (95%)
  local copies, waits for them, and re-layouts  2.88 us (4%)
    pallas_call x1, Pallas kernels, body(): pl.pallas_call(functools.partial(kernel, n, pieces), out_shape=(jax.Shape...  71.1 us
    unnamed x4, local copies, waits for them, and re-layouts  2.88 us

profile of v4, /device:TPU:0, one launch (start us, length us, event | category | flops | bytes accessed | tf_op | source)
XLA Modules:
  0.0 74.7 jit_solution(12604573471681175986)
XLA Ops:
  0.6 71.1 %shard_map.68 = (f32[3,768,128]{2,1,0:T(8,128)}, f32[1,128]{1,0:T(1,128)}) custom-call(f32[3,768,128]{2,1,0:T(8,128)} %rhs.1, f32[768]{0:T(1024)} %weight.1, s32[2,2]{1,0:T(2,128)} %bitcast.2, f32[3,768,768]{2,1,0:T(8,128)} %diag.1, f32[2,2,768,768]{3,2,1,0:T(8,128)} %tiles.1), custom_call_target="tpu_custom_call" | custom-call | flops 3170893824 | bytes 16515072 | tf_op jit(solution)/shard_map/pallas_call | solution.py:352
  71.8 0.0 copy-start
  71.8 2.4 %copy.9 = f32[3,768,128]{2,1,0:T(8,128)} copy(f32[3,768,128]{2,1,0:T(8,128)} %get-tuple-element.8) | data formatting | bytes 2359296
  74.1 0.0 copy-done
  74.2 0.5 copy.10
Async XLA Ops:
  71.8 2.4 %copy-start = (f32[1,128]{1,0:T(1,128)S(1)}, f32[1,128]{1,0:T(1,128)}, u32[]{:S(2)}) copy-start(f32[1,128]{1,0:T(1,128)} %get-tuple-element.5) | copy-start | bytes 1540

commit v5 on v4

--- a/solution.py
+++ b/solution.py
@@ -26,19 +26,16 @@
         n_send, n_recv, n_copy, o_send, o_recv,
     ) = scratch[4 * pieces :]
     size, width = rhs.shape[1], rhs.shape[2]
-    half, hubs = n // 2, n // 4
+    half = n // 2
     block = size // pieces
     packed = block // 2
-    rows = packed // hubs
+    rows = packed // half
     me = lax.axis_index("rows")
     side = me // half
     base = side * half
     pos = me - base
-    first_hub = (1 - side) * hubs
-    is_hub = jnp.logical_and(pos >= first_hub, pos < first_hub + hubs)
-    hub = pos - first_hub
     opposite = (1 - side) * half
-    peer = me + hubs * (1 - 2 * side)
+    peer = me + half * (1 - 2 * side)
 
     barrier = pltpu.get_barrier_semaphore()
     for j in range(1, n):
@@ -127,14 +124,14 @@
     def names_copy(to):
         return pltpu.make_async_remote_copy(
             src_ref=share, dst_ref=names.at[pos], send_sem=n_send, recv_sem=n_recv,
-            device_id={"rows": base + first_hub + to})
+            device_id={"rows": base + to})
 
     def first(p, c, to):
         return pltpu.make_async_remote_copy(
             src_ref=send1.at[p, c, :, pl.ds(pl.multiple_of(to * rows, rows), rows), :],
             dst_ref=stage1[p][c].at[pl.ds(2 * pos, 2)],
             send_sem=s1_send.at[p], recv_sem=s1_recv.at[p, c],
-            device_id={"rows": base + first_hub + to})
+            device_id={"rows": base + to})
 
     def second(p, c):
         return pltpu.make_async_remote_copy(
@@ -142,7 +139,7 @@
             send_sem=s2_send.at[p, c], recv_sem=s2_recv.at[p, c], device_id={"rows": peer})
 
     def third(p, c, owner):
-        at = pl.ds(pl.multiple_of(hub * rows, rows), rows)
+        at = pl.ds(pl.multiple_of(pos * rows, rows), rows)
         return pltpu.make_async_remote_copy(
             src_ref=send3.at[p, c, owner], dst_ref=update.at[p, c, at, :],
             send_sem=s3_send.at[p], recv_sem=s3_recv.at[p],
@@ -158,17 +155,12 @@
                 value = multiply(tile_hi[t, k, at, :], tile_lo[t, k, at, :], h)
                 top, bottom = value[:packed], value[packed:]
                 send1[p, c, k] = jnp.where(left(top.shape), top, bottom)
-            @pl.when(is_hub)
-            def _():
-                at = pl.ds(pl.multiple_of(hub * rows, rows), rows)
-                stage1[p][c][pl.ds(2 * pos, 2)] = send1[p, c, :, at, :]
-
-            @pl.when(jnp.logical_not(is_hub))
-            def _():
-                first(p, c, lax.rem(pos, hubs)).start()
-
-            for j in range(1, hubs):
-                first(p, c, lax.rem(pos + j, hubs)).start()
+            at = pl.ds(pl.multiple_of(pos * rows, rows), rows)
+            stage1[p][c][pl.ds(2 * pos, 2)] = send1[p, c, :, at, :]
+
+
+            for j in range(1, half):
+                first(p, c, lax.rem(pos + j, half)).start()
 
     def build_table():
         await_bytes(names.at[pl.ds(0, half - 1)], n_recv)
@@ -195,9 +187,7 @@
             out[i] = total + (buffer[table[d, column + 2]] + buffer[table[d, column + 3]])
 
     def give_back(step):
-        @pl.when(is_hub)
-        def _():
-            finish(step)
+        finish(step)
 
     def finish(step):
         p, c = step // pieces, step % pieces
@@ -207,29 +197,22 @@
             send3[p, c, i] = own[step % OWN, i] + recv2[p, c, i]
         for j in range(1, half):
             third(p, c, lax.rem(pos + j, half)).start()
-        update[p, c, pl.ds(pl.multiple_of(hub * rows, rows), rows), :] = send3[p, c, pos]
+        update[p, c, pl.ds(pl.multiple_of(pos * rows, rows), rows), :] = send3[p, c, pos]
 
     def gather(step):
         p, c = step // pieces, step % pieces
 
-        @pl.when(is_hub)
-        def _():
-            if step == 0:
-                build_table()
-            await_bytes(stage1[p][c].at[pl.ds(0, 2 * (half - 1))], s1_recv.at[p, c])
-            add_up(p, c, opposite, send2.at[p, c])
-            second(p, c).start()
-            add_up(p, c, base, own.at[step % OWN])
+        if step == 0:
+            build_table()
+        await_bytes(stage1[p][c].at[pl.ds(0, 2 * (half - 1))], s1_recv.at[p, c])
+        add_up(p, c, opposite, send2.at[p, c])
+        second(p, c).start()
+        add_up(p, c, base, own.at[step % OWN])
 
     def receive(p):
         t, h = p // 2, p % 2
-        @pl.when(is_hub)
-        def _():
-            await_bytes(update.at[p, :, pl.ds(0, packed - rows), :], s3_recv.at[p])
-
-        @pl.when(jnp.logical_not(is_hub))
-        def _():
-            await_bytes(update.at[p], s3_recv.at[p])
+        await_bytes(update.at[p, :, pl.ds(0, packed - rows), :], s3_recv.at[p])
+
 
         parts = []
         for c in range(pieces):
@@ -251,16 +234,11 @@
     split_diag(0, 0, size)
     solve(0, 0, twice(rhs_v[0], 0))
     pl.semaphore_wait(barrier, n - 1)
-    @pl.when(is_hub)
-    def _():
-        names[pos] = share[...]
-
-    @pl.when(jnp.logical_not(is_hub))
-    def _():
-        names_copy(lax.rem(pos, hubs)).start()
-
-    for j in range(1, hubs):
-        names_copy(lax.rem(pos + j, hubs)).start()
+    names[pos] = share[...]
+
+
+    for j in range(1, half):
+        names_copy(lax.rem(pos + j, half)).start()
     await_tiles(0)
     for copy in loads[4:]:
         copy.start()
@@ -313,20 +291,12 @@
             src_ref=shares.at[me], dst_ref=shares.at[me], send_sem=o_send,
             recv_sem=o_recv, device_id={"rows": lax.rem(me + j, n)}).start()
 
-    @pl.when(is_hub)
-    def _():
-        await_bytes(names.at[pl.ds(0, hubs - 1)], n_send)
-        for p in range(4):
-            await_bytes(send1.at[p, :, :, pl.ds(0, packed - rows), :], s1_send.at[p])
-            await_bytes(send3.at[p, :, pl.ds(0, half - 1)], s3_send.at[p])
-            for c in range(pieces):
-                second(p, c).wait_send()
-
-    @pl.when(jnp.logical_not(is_hub))
-    def _():
-        await_bytes(names.at[pl.ds(0, hubs)], n_send)
-        for p in range(4):
-            await_bytes(send1.at[p], s1_send.at[p])
+    await_bytes(names.at[pl.ds(0, half - 1)], n_send)
+    for p in range(4):
+        await_bytes(send1.at[p, :, :, pl.ds(0, packed - rows), :], s1_send.at[p])
+        await_bytes(send3.at[p, :, pl.ds(0, half - 1)], s3_send.at[p])
+        for c in range(pieces):
+            second(p, c).wait_send()
 
     await_bytes(shares.at[pl.ds(0, n - 1)], o_send)
     await_bytes(shares.at[pl.ds(0, n - 1)], o_recv)
@@ -341,10 +311,10 @@
 def body(rhs, diag_inv, tiles, dest, obs_weight):
     n = lax.axis_size("rows")
     size, width = rhs.shape[1], rhs.shape[2]
-    half, hubs = n // 2, n // 4
+    half = n // 2
     pieces = PIECES
     packed = size // pieces // 2
-    rows = packed // hubs
+    rows = packed // half
     f32, bf16 = jnp.float32, jnp.bfloat16
     dma = pltpu.SemaphoreType.DMA
     vmem = pl.BlockSpec(memory_space=pltpu.VMEM)

time: 74.9 us -> 75.9 us (1.013)
  Pallas kernels: 71.1 us -> 72.1 us
    pallas_call x1, Pallas kernels: 71.1 us -> 72.1 us  [body(): pl.pallas_call(functools.partial(kernel, n, pieces), out_shape=(jax.Shape...]
where the time goes in v5:
time: 75.9 us; the launch traced here: 75.7 us
  Pallas kernels  72.1 us (95%)
  local copies, waits for them, and re-layouts  2.88 us (4%)
    pallas_call x1, Pallas kernels, body(): pl.pallas_call(functools.partial(kernel, n, pieces), out_shape=(jax.Shape...  72.1 us
    unnamed x4, local copies, waits for them, and re-layouts  2.88 us

profile of v5, /device:TPU:0, one launch (start us, length us, event | category | flops | bytes accessed | tf_op | source)
XLA Modules:
  0.0 75.7 jit_solution(2692669651942541672)
XLA Ops:
  0.6 72.1 %shard_map.68 = (f32[3,768,128]{2,1,0:T(8,128)}, f32[1,128]{1,0:T(1,128)}) custom-call(f32[3,768,128]{2,1,0:T(8,128)} %rhs.1, f32[768]{0:T(1024)} %weight.1, s32[2,2]{1,0:T(2,128)} %bitcast.2, f32[3,768,768]{2,1,0:T(8,128)} %diag.1, f32[2,2,768,768]{3,2,1,0:T(8,128)} %tiles.1), custom_call_target="tpu_custom_call" | custom-call | flops 3170893824 | bytes 16515072 | tf_op jit(solution)/shard_map/pallas_call | solution.py:322
  72.8 0.0 copy-start
  72.8 2.4 %copy.9 = f32[3,768,128]{2,1,0:T(8,128)} copy(f32[3,768,128]{2,1,0:T(8,128)} %get-tuple-element.8) | data formatting | bytes 2359296
  75.2 0.0 copy-done
  75.2 0.5 copy.10
Async XLA Ops:
  72.8 2.4 %copy-start = (f32[1,128]{1,0:T(1,128)S(1)}, f32[1,128]{1,0:T(1,128)}, u32[]{:S(2)}) copy-start(f32[1,128]{1,0:T(1,128)} %get-tuple-element.5) | copy-start | bytes 1540

commit v6 on v4

--- a/solution.py
+++ b/solution.py
@@ -8,13 +8,27 @@
 from jax.sharding import PartitionSpec as P
 
 CAP = 4
-PIECES = 3
-OWN = 4
+PIECES = 6
 
 
 def split(value):
     high = value.astype(jnp.bfloat16)
     return high, (value - high.astype(jnp.float32)).astype(jnp.bfloat16)
+
+
+def order_of_work(pieces):
+    span = 8.0
+    begin, events = [0.0, span], []
+    for p in range(4):
+        for c in range(pieces):
+            at = begin[p] + (c + 1) * span / pieces
+            events.append((at, "gather", p * pieces + c))
+            events.append((at + 3.5, "return", p * pieces + c))
+        ready = begin[p] + span + 6.5
+        events.append((ready, "solve", p))
+        if p < 2:
+            begin.append(max(ready + 3.0, begin[-1] + span))
+    return [event[1:] for event in sorted(events)]
 
 
 def kernel(n, pieces, rhs, weight, dest, diag, tiles, sol, observed, *scratch):
@@ -204,7 +218,7 @@
         second(p, c).wait_recv()
 
         for i in range(half):
-            send3[p, c, i] = own[step % OWN, i] + recv2[p, c, i]
+            send3[p, c, i] = own[step, i] + recv2[p, c, i]
         for j in range(1, half):
             third(p, c, lax.rem(pos + j, half)).start()
         update[p, c, pl.ds(pl.multiple_of(hub * rows, rows), rows), :] = send3[p, c, pos]
@@ -219,7 +233,7 @@
             await_bytes(stage1[p][c].at[pl.ds(0, 2 * (half - 1))], s1_recv.at[p, c])
             add_up(p, c, opposite, send2.at[p, c])
             second(p, c).start()
-            add_up(p, c, base, own.at[step % OWN])
+            add_up(p, c, base, own.at[step])
 
     def receive(p):
         t, h = p // 2, p % 2
@@ -269,38 +283,25 @@
     result_copy(0).start()
     send_products(1)
 
-    gather(0)
-    await_diag(1)
-    split_diag(1, 0, size)
-    await_tiles(1)
-    split_tiles(1, 0, size)
-    for step in range(1, pieces + 1):
-        gather(step)
-        give_back(step - 1)
-    for step in range(pieces + 1, 2 * pieces):
-        gather(step)
-        if step < 2 * pieces - 1:
-            give_back(step - 1)
-    receive(0)
-    send_products(2)
-    for step in range(2 * pieces - 2, 2 * pieces):
-        give_back(step)
-    await_diag(2)
-    split_diag(2, 0, size)
-    gather(2 * pieces)
-    receive(1)
-    result_copy(1).start()
-    send_products(3)
-    for step in range(2 * pieces + 1, 3 * pieces + 1):
-        gather(step)
-        give_back(step - 1)
-    for step in range(3 * pieces + 1, 4 * pieces):
-        gather(step)
-        if step < 4 * pieces - 1:
-            give_back(step - 1)
-    receive(2)
-    for step in range(4 * pieces - 2, 4 * pieces):
-        give_back(step)
+    for kind, item in order_of_work(pieces):
+        if kind == "gather":
+            gather(item)
+            if item == 0:
+                await_diag(1)
+                split_diag(1, 0, size)
+                await_tiles(1)
+                split_tiles(1, 0, size)
+            if item == 2 * pieces:
+                await_diag(2)
+                split_diag(2, 0, size)
+        elif kind == "return":
+            give_back(item)
+        elif item < 3:
+            receive(item)
+            if item == 1:
+                result_copy(1).start()
+            if item < 2:
+                send_products(item + 2)
     receive(3)
     result_copy(2).start()
 
@@ -370,7 +371,7 @@
             pltpu.VMEM((4, pieces, 2, packed, width), f32),
             pltpu.VMEM((4, pieces, half, rows, width), f32),
             pltpu.VMEM((4, pieces, half, rows, width), f32),
-            pltpu.VMEM((OWN, half, rows, width), f32),
+            pltpu.VMEM((4 * pieces, half, rows, width), f32),
             pltpu.VMEM((4, pieces, half, rows, width), f32),
             pltpu.VMEM((4, pieces, packed, width), f32),
             pltpu.VMEM((8, 128), jnp.int32),

time: 74.9 us -> 75.1 us (level)
  no operation moved by 1% of the time
where the time goes in v6:
time: 75.1 us; the launch traced here: 74.9 us
  Pallas kernels  71.4 us (95%)
  local copies, waits for them, and re-layouts  2.88 us (4%)
    pallas_call x1, Pallas kernels, body(): pl.pallas_call(functools.partial(kernel, n, pieces), out_shape=(jax.Shape...  71.4 us
    unnamed x4, local copies, waits for them, and re-layouts  2.88 us

profile of v6, /device:TPU:0, one launch (start us, length us, event | category | flops | bytes accessed | tf_op | source)
XLA Modules:
  0.0 74.9 jit_solution(7823193500828870769)
XLA Ops:
  0.6 71.4 %shard_map.68 = (f32[3,768,128]{2,1,0:T(8,128)}, f32[1,128]{1,0:T(1,128)}) custom-call(f32[3,768,128]{2,1,0:T(8,128)} %rhs.1, f32[768]{0:T(1024)} %weight.1, s32[2,2]{1,0:T(2,128)} %bitcast.2, f32[3,768,768]{2,1,0:T(8,128)} %diag.1, f32[2,2,768,768]{3,2,1,0:T(8,128)} %tiles.1), custom_call_target="tpu_custom_call" | custom-call | flops 3170893824 | bytes 16515072 | tf_op jit(solution)/shard_map/pallas_call | solution.py:353
  72.1 0.0 copy-start
  72.1 2.4 %copy.9 = f32[3,768,128]{2,1,0:T(8,128)} copy(f32[3,768,128]{2,1,0:T(8,128)} %get-tuple-element.8) | data formatting | bytes 2359296
  74.4 0.0 copy-done
  74.4 0.5 copy.10
Async XLA Ops:
  72.1 2.4 %copy-start = (f32[1,128]{1,0:T(1,128)S(1)}, f32[1,128]{1,0:T(1,128)}, u32[]{:S(2)}) copy-start(f32[1,128]{1,0:T(1,128)} %get-tuple-element.5) | copy-start | bytes 1540

commit v7 on v3

--- a/solution.py
+++ b/solution.py
@@ -114,6 +114,16 @@
             mixed = jnp.where(left(value.shape), rhs_v[level], value)
         rhs_v[level] = mixed
 
+    def keep_all(value):
+        high, low = split(value)
+        solved[0, :, :width] = high
+        solved[0, :, width:] = low
+
+    def multiply_all(high, low):
+        wide = jnp.dot(high, solved[0], preferred_element_type=jnp.float32)
+        other = jnp.dot(low, solved[0, :, :width], preferred_element_type=jnp.float32)
+        return wide[:, :width] + wide[:, width:] + other
+
     def result_copy(level):
         return pltpu.make_async_copy(rhs_v.at[level], sol.at[level], out_sem.at[level])
 
@@ -141,6 +151,19 @@
             send_sem=s3_send.at[p], recv_sem=s3_recv.at[p],
             device_id={"rows": base + owner})
 
+    def send_piece(p, c):
+        @pl.when(is_hub)
+        def _():
+            at = pl.ds(pl.multiple_of(hub * rows, rows), rows)
+            stage1[p][c][pl.ds(2 * pos, 2)] = send1[p, c, :, at, :]
+
+        @pl.when(jnp.logical_not(is_hub))
+        def _():
+            first(p, c, lax.rem(pos, hubs)).start()
+
+        for j in range(1, hubs):
+            first(p, c, lax.rem(pos + j, hubs)).start()
+
     def send_products(p):
         t, h = p // 2, p % 2
         for c in range(pieces):
@@ -149,17 +172,28 @@
                 value = multiply(tile_hi[t, k, at, :], tile_lo[t, k, at, :], h)
                 top, bottom = value[:packed], value[packed:]
                 send1[p, c, k] = jnp.where(left(top.shape), top, bottom)
-            @pl.when(is_hub)
-            def _():
-                at = pl.ds(pl.multiple_of(hub * rows, rows), rows)
-                stage1[p][c][pl.ds(2 * pos, 2)] = send1[p, c, :, at, :]
-
-            @pl.when(jnp.logical_not(is_hub))
-            def _():
-                first(p, c, lax.rem(pos, hubs)).start()
-
-            for j in range(1, hubs):
-                first(p, c, lax.rem(pos + j, hubs)).start()
+            send_piece(p, c)
+
+    def first_level():
+        keep_all(rhs_v[0])
+        for c in range(pieces):
+            at = pl.ds(c * block, block)
+            rhs_v[0, at, :] = multiply_all(diag_hi[0, at, :], diag_lo[0, at, :])
+        result_copy(0).start()
+        keep_all(rhs_v[0])
+
+    def first_products():
+        for c in range(pieces):
+            at = pl.ds(c * block, block)
+            for k in range(2):
+                value = multiply_all(tile_hi[0, k, at, :], tile_lo[0, k, at, :])
+                top, bottom = value[:packed], value[packed:]
+                mask = left(top.shape)
+                send1[0, c, k] = jnp.where(mask, top, swap(bottom))
+                send1[1, c, k] = jnp.where(mask, swap(top), bottom)
+            send_piece(0, c)
+        for c in range(pieces):
+            send_piece(1, c)
 
     def build_table():
         await_bytes(names.at[pl.ds(0, half - 1)], n_recv)
@@ -237,7 +271,7 @@
             stage1[p][c][n] = jnp.zeros((rows, width), jnp.float32)
 
     ready_diag(0)
-    solve(0, 0, twice(rhs_v[0], 0))
+    first_level()
     pl.semaphore_wait(barrier, n - 1)
     @pl.when(is_hub)
     def _():
@@ -252,10 +286,7 @@
     ready_tiles(0)
     for copy in loads[4:]:
         copy.start()
-    send_products(0)
-    solve(0, 1, twice(rhs_v[0], 1))
-    result_copy(0).start()
-    send_products(1)
+    first_products()
 
     for step in range(4 * pieces + 1):
         hub_step(step)
@@ -308,6 +339,33 @@
     observed[...] = total[:1]
     for level in range(3):
         result_copy(level).wait()
+
+
+def hand_over_kernel(parts, source, target, sem):
+    levels, size = source.shape[:2]
+    step = size // parts
+    copies = [
+        pltpu.make_async_copy(
+            source.at[level, pl.ds(i * step, step), :], target.at[level, pl.ds(i * step, step), :],
+            sem.at[level * parts + i])
+        for level in range(levels) for i in range(parts)
+    ]
+    for copy in copies:
+        copy.start()
+    for copy in copies:
+        copy.wait()
+
+
+def hand_over(value):
+    parts = 4
+    return pl.pallas_call(
+        functools.partial(hand_over_kernel, parts),
+        out_shape=jax.ShapeDtypeStruct(value.shape, value.dtype),
+        in_specs=[pl.BlockSpec(memory_space=pl.ANY)],
+        out_specs=pl.BlockSpec(memory_space=pl.ANY),
+        scratch_shapes=[pltpu.SemaphoreType.DMA((value.shape[0] * parts,))],
+        cost_estimate=pl.CostEstimate(flops=0, bytes_accessed=8 * value.size, transcendentals=0),
+    )(value)
 
 
 def body(rhs, diag_inv, tiles, dest, obs_weight):
@@ -363,7 +421,7 @@
             flops=7 * 3 * 2 * size * size * width, bytes_accessed=7 * 4 * size * size, transcendentals=0
         ),
     )(rhs, obs_weight, dest.reshape(2, 2), diag_inv, tiles)
-    return sol, observed.reshape(width)
+    return hand_over(sol), observed.reshape(width)
 
 
 def solution(mesh):

time: 74.3 us -> 109 us (1.47)
  Pallas kernels: 70.5 us -> 107 us
  local copies, waits for them, and re-layouts: 2.88 us -> 0.52 us
    pallas_call x0 -> x1, Pallas kernels: none -> 36.9 us  [hand_over(): pl.pallas_call(functools.partial(hand_over_kernel, parts), out_shape=jax....]
    unnamed x4 -> x3, local copies, waits for them, and re-layouts: 2.88 us -> 0.52 us
where the time goes in v7:
time: 109 us
  Pallas kernels  107 us (98%)
    pallas_call x1, Pallas kernels, body(): pl.pallas_call(functools.partial(kernel, n, pieces), out_shape=(jax.Shape...  70.5 us
    pallas_call x1, Pallas kernels, hand_over(): pl.pallas_call(functools.partial(hand_over_kernel, parts), out_shape=jax....  36.9 us

profile of v7, /device:TPU:0, one launch (start us, length us, event | category | flops | bytes accessed | tf_op | source)
XLA Modules:
  0.0 108.6 jit_solution(14375685795841955644)
XLA Ops:
  0.6 70.5 %shard_map.68 = (f32[3,768,128]{2,1,0:T(8,128)}, f32[1,128]{1,0:T(1,128)}) custom-call(f32[3,768,128]{2,1,0:T(8,128)} %rhs.1, f32[768]{0:T(1024)} %weight.1, s32[2,2]{1,0:T(2,128)} %bitcast.2, f32[3,768,768]{2,1,0:T(8,128)} %diag.1, f32[2,2,768,768]{3,2,1,0:T(8,128)} %tiles.1), custom_call_target="tpu_custom_call" | custom-call | flops 3170893824 | bytes 16515072 | tf_op jit(solution)/shard_map/pallas_call | solution.py:382
  71.1 0.0 copy-start
  71.1 36.9 %shard_map.69 = f32[3,768,128]{2,1,0:T(8,128)} custom-call(f32[3,768,128]{2,1,0:T(8,128)} %get-tuple-element.4.source), custom_call_target="tpu_custom_call" | custom-call | bytes 2359296 | tf_op jit(solution)/shard_map/pallas_call | solution.py:361
  108.1 0.0 copy-done
  108.1 0.5 copy.8
Async XLA Ops:
  71.1 37.0 %copy-start = (f32[1,128]{1,0:T(1,128)S(1)}, f32[1,128]{1,0:T(1,128)}, u32[]{:S(2)}) copy-start(f32[1,128]{1,0:T(1,128)} %get-tuple-element.5) | copy-start | bytes 1540
